TPU v7x, 256 devices: a whole 4x4x8 slice. The times are simulated.
256 devices in a mesh: src: 8 (over y, core), tgt: 32 (over x, z).
Axes of the slice: x: 4, y: 4, z: 8, core: 2. Of those that a mesh axis runs over, the one named last changes fastest.
Arguments:
- source: bfloat16 [16384, 128], P('src'), may hold values from -6 to 6
- target: bfloat16 [32768, 128], P('tgt'), may hold values from -5 to 5
- start_map: float32 [128, 128], replicated, may hold values from -1 to 1
- warm_potential: float32 [32768], P('tgt'), may hold values from -60 to 24
Outputs:
- row_potential: float32 [16384], P('src')
- col_potential: float32 [32768], P('tgt')
- new_map: float32 [128, 128], replicated
All inputs are finite; a program needn't handle non-finite values.
Results may differ from a plain program's by a relative error of at most 0.0078.
Values sent between devices are 32-bit elements; how exact they have to be, the bound alone decides.
A program may use at most 64 MiB of HBM per device.

v0:
```python
import math
import jax
import jax.numpy as jnp
from jax import lax
from jax.sharding import PartitionSpec as P

ROUNDS = 3
NEWTON = 10
EPS = 0.05


def row_partials(rotated, target, col_pot, score_scale):
    row_count = rotated.shape[0]
    block_rows = math.gcd(row_count, 512)
    blocks = rotated.reshape(row_count // block_rows, block_rows, rotated.shape[1])

    def row_one_block(row_block):
        scores = (
            jnp.einsum("rd,cd->rc", row_block, target, preferred_element_type=jnp.float32)
            * score_scale
            + col_pot[None, :]
        )
        peak_val = jnp.max(scores, axis=1)
        totals = jnp.sum(jnp.exp(scores - peak_val[:, None]), axis=1)
        return (peak_val, totals)

    peak_val, totals = lax.map(row_one_block, blocks)
    return (peak_val.reshape(row_count), totals.reshape(row_count))


def col_partials(rotated, target, row_pot, score_scale):
    row_count = rotated.shape[0]
    block_rows = math.gcd(row_count, 512)
    blocks = rotated.reshape(row_count // block_rows, block_rows, rotated.shape[1])
    pots = row_pot.reshape(row_count // block_rows, block_rows)

    def col_one_block(inputs):
        row_block, pot_block = inputs
        scores = (
            jnp.einsum("rd,cd->rc", row_block, target, preferred_element_type=jnp.float32)
            * score_scale
            + pot_block[:, None]
        )
        peak_val = jnp.max(scores, axis=0)
        totals = jnp.sum(jnp.exp(scores - peak_val[None, :]), axis=0)
        return (peak_val, totals)

    peaks, totals = lax.map(col_one_block, (blocks, pots))
    peak_val = jnp.max(peaks, axis=0)
    return (peak_val, jnp.sum(totals * jnp.exp(peaks - peak_val[None, :]), axis=0))


def across_targets(peak_val, totals):
    global_peak = lax.pmax(peak_val, "tgt")
    totals = lax.psum(totals * jnp.exp(peak_val - global_peak), "tgt")
    peak_val = global_peak
    return peak_val + jnp.log(totals)


def across_sources(peak_val, totals):
    global_peak = lax.pmax(peak_val, "src")
    totals = lax.psum(totals * jnp.exp(peak_val - global_peak), "src")
    peak_val = global_peak
    return peak_val + jnp.log(totals)


def polar(matrix):
    iterate = matrix / jnp.sqrt(jnp.sum(matrix * matrix) + 1e-06)
    for newton_index in range(NEWTON):
        gram_matrix = jnp.dot(iterate.T, iterate, precision=lax.Precision.HIGHEST)
        iterate = 1.5 * iterate - 0.5 * jnp.dot(
            iterate, gram_matrix, precision=lax.Precision.HIGHEST
        )
    return iterate


def shards(source, target, start_map, warm_potential):
    width = source.shape[1]
    score_scale = 1.0 / (math.sqrt(width) * EPS)
    rows_all = source.shape[0] * lax.axis_size("src")
    cols_all = target.shape[0] * lax.axis_size("tgt")
    rotated = jnp.dot(
        source, start_map.astype(jnp.bfloat16), preferred_element_type=jnp.float32
    ).astype(jnp.bfloat16)
    col_pot = warm_potential
    for round_index in range(ROUNDS):
        row_pot = -math.log(rows_all) - across_targets(
            *row_partials(rotated, target, col_pot, score_scale)
        )
        col_pot = -math.log(cols_all) - across_sources(
            *col_partials(rotated, target, row_pot, score_scale)
        )
    row_lse = across_targets(*row_partials(rotated, target, col_pot, score_scale))
    row_pot = -math.log(rows_all) - row_lse
    rows_here = source.shape[0] // lax.axis_size("tgt")
    block_rows = math.gcd(rows_here * lax.axis_size("tgt"), 512)
    nblocks = rows_here * lax.axis_size("tgt") // block_rows

    def numerator_one_block(inputs):
        row_block, lse_block = inputs
        scores = (
            jnp.einsum("rd,cd->rc", row_block, target, preferred_element_type=jnp.float32)
            * score_scale
            + col_pot[None, :]
            - lse_block[:, None]
        )
        weights = jnp.exp(scores).astype(jnp.bfloat16)
        return jnp.dot(weights, target, preferred_element_type=jnp.float32)

    parts_out = lax.map(
        numerator_one_block,
        (rotated.reshape(nblocks, block_rows, width), row_lse.reshape(nblocks, block_rows)),
    )
    my_targets = lax.psum_scatter(
        parts_out.reshape(rows_here * lax.axis_size("tgt"), width),
        "tgt",
        scatter_dimension=0,
        tiled=True,
    )
    source_rows = lax.dynamic_slice_in_dim(source, lax.axis_index("tgt") * rows_here, rows_here, 0)
    partial_value = jnp.einsum(
        "rd,re->de", source_rows.astype(jnp.float32), my_targets, precision=lax.Precision.HIGHEST
    )
    covariance_sum = lax.psum(partial_value, ("src", "tgt"))
    new_map = polar(covariance_sum)
    return (EPS * row_pot, EPS * col_pot, new_map)


def solution(mesh):
    placed = (P("src", None), P("tgt", None), P(), P("tgt"))
    return jax.shard_map(
        shards, mesh=mesh, in_specs=placed, out_specs=(P("src"), P("tgt"), P()), check_vma=False
    )
```

profile of v0, /device:TPU:1, one launch (start us, length us, event | category | flops | bytes accessed | tf_op | source)
XLA Modules:
  0.0 1202.2 jit_solution(3626454813866031106)
XLA Ops:
  9.4 8.7 while.94
  9.4 1.5 fusion.139
  11.6 1.5 fusion.139
  13.7 1.5 fusion.139
  15.9 1.5 fusion.139
  18.1 65.3 %pmax.49 = f32[2048]{0:T(1024)S(1)} all-reduce(f32[2048]{0:T(1024)S(1)} %bitcast.221), channel_id=1, replica_groups=mesh['src'=8,'tgt'=32] {'tgt'}, use_global_device_ids=true, to_apply=%region_4.5 | all-reduce | flops 2048 | bytes 16384 | tf_op jit(solution)/shard_map/pmax | solution.py:54
  83.4 56.8 %psum.56 = f32[2048]{0:T(1024)S(1)} all-reduce(f32[2048]{0:T(1024)S(1)} %exponential_multiply_fusion.3), channel_id=1, replica_groups=mesh['src'=8,'tgt'=32] {'tgt'}, use_global_device_ids=true, to_apply=%region_5.6 | all-reduce | flops 2048 | bytes 16384 | tf_op jit(solution)/shard_map/psum | solution.py:55
  140.3 8.4 while.95
  146.6 1.4 fusion.141
  148.7 40.6 %pmax.50 = f32[1024]{0:T(1024)S(1)} all-reduce(f32[1024]{0:T(1024)S(1)} %reduce_max.90), channel_id=1, replica_groups=mesh['src'=8,'tgt'=32] {'src'}, use_global_device_ids=true, to_apply=%region_11.12 | all-reduce | flops 1024 | bytes 8192 | tf_op jit(solution)/shard_map/pmax | solution.py:61
  189.4 12.3 %psum.57 = f32[1024]{0:T(1024)S(1)} all-reduce(f32[1024]{0:T(1024)S(1)} %exponential_multiply_fusion.6), channel_id=1, replica_groups=mesh['src'=8,'tgt'=32] {'src'}, use_global_device_ids=true, to_apply=%region_13.14 | all-reduce | flops 1024 | bytes 8192 | tf_op jit(solution)/shard_map/psum | solution.py:62
  201.7 8.7 while.96
  201.7 1.5 fusion.143
  203.9 1.5 fusion.143
  206.1 1.5 fusion.143
  208.2 1.5 fusion.143
  210.4 58.5 %pmax.51 = f32[2048]{0:T(1024)S(1)} all-reduce(f32[2048]{0:T(1024)S(1)} %bitcast.223), channel_id=1, replica_groups=mesh['src'=8,'tgt'=32] {'tgt'}, use_global_device_ids=true, to_apply=%region_18.19 | all-reduce | flops 2048 | bytes 16384 | tf_op jit(solution)/shard_map/pmax | solution.py:54
  268.9 56.8 %psum.58 = f32[2048]{0:T(1024)S(1)} all-reduce(f32[2048]{0:T(1024)S(1)} %exponential_multiply_fusion.2), channel_id=1, replica_groups=mesh['src'=8,'tgt'=32] {'tgt'}, use_global_device_ids=true, to_apply=%region_19.20 | all-reduce | flops 2048 | bytes 16384 | tf_op jit(solution)/shard_map/psum | solution.py:55
  325.8 8.4 while.97
  332.1 1.4 fusion.145
  334.2 40.5 %pmax.52 = f32[1024]{0:T(1024)S(1)} all-reduce(f32[1024]{0:T(1024)S(1)} %reduce_max.91), channel_id=1, replica_groups=mesh['src'=8,'tgt'=32] {'src'}, use_global_device_ids=true, to_apply=%region_25.26 | all-reduce | flops 1024 | bytes 8192 | tf_op jit(solution)/shard_map/pmax | solution.py:61
  374.8 12.4 %psum.59 = f32[1024]{0:T(1024)S(1)} all-reduce(f32[1024]{0:T(1024)S(1)} %exponential_multiply_fusion.5), channel_id=1, replica_groups=mesh['src'=8,'tgt'=32] {'src'}, use_global_device_ids=true, to_apply=%region_27.28 | all-reduce | flops 1024 | bytes 8192 | tf_op jit(solution)/shard_map/psum | solution.py:62
  387.2 8.7 while.98
  387.2 1.5 fusion.147
  389.4 1.5 fusion.147
  391.6 1.5 fusion.147
  393.8 1.5 fusion.147
  395.9 59.2 %pmax.53 = f32[2048]{0:T(1024)S(1)} all-reduce(f32[2048]{0:T(1024)S(1)} %bitcast.225), channel_id=1, replica_groups=mesh['src'=8,'tgt'=32] {'tgt'}, use_global_device_ids=true, to_apply=%region_32.33 | all-reduce | flops 2048 | bytes 16384 | tf_op jit(solution)/shard_map/pmax | solution.py:54
  455.1 57.0 %psum.60 = f32[2048]{0:T(1024)S(1)} all-reduce(f32[2048]{0:T(1024)S(1)} %exponential_multiply_fusion.1), channel_id=1, replica_groups=mesh['src'=8,'tgt'=32] {'tgt'}, use_global_device_ids=true, to_apply=%region_33.34 | all-reduce | flops 2048 | bytes 16384 | tf_op jit(solution)/shard_map/psum | solution.py:55
  512.2 8.4 while.99
  520.6 39.6 %pmax.54 = f32[1024]{0:T(1024)S(1)} all-reduce(f32[1024]{0:T(1024)S(1)} %reduce_max.92), channel_id=1, replica_groups=mesh['src'=8,'tgt'=32] {'src'}, use_global_device_ids=true, to_apply=%region_39.40 | all-reduce | flops 1024 | bytes 8192 | tf_op jit(solution)/shard_map/pmax | solution.py:61
  560.3 12.4 %psum.61 = f32[1024]{0:T(1024)S(1)} all-reduce(f32[1024]{0:T(1024)S(1)} %exponential_multiply_fusion.4), channel_id=1, replica_groups=mesh['src'=8,'tgt'=32] {'src'}, use_global_device_ids=true, to_apply=%region_41.42 | all-reduce | flops 1024 | bytes 8192 | tf_op jit(solution)/shard_map/psum | solution.py:62
  573.3 8.7 while.100
  573.3 1.5 fusion.151
  575.5 1.5 fusion.151
  577.7 1.5 fusion.151
  579.9 1.5 fusion.151
  582.1 59.2 %pmax.55 = f32[2048]{0:T(1024)S(1)} all-reduce(f32[2048]{0:T(1024)S(1)} %bitcast.227), channel_id=1, replica_groups=mesh['src'=8,'tgt'=32] {'tgt'}, use_global_device_ids=true, to_apply=%region_46.47 | all-reduce | flops 2048 | bytes 16384 | tf_op jit(solution)/shard_map/pmax | solution.py:54
  641.3 57.0 %psum.62 = f32[2048]{0:T(1024)S(1)} all-reduce(f32[2048]{0:T(1024)S(1)} %exponential_multiply_fusion), channel_id=1, replica_groups=mesh['src'=8,'tgt'=32] {'tgt'}, use_global_device_ids=true, to_apply=%region_47.48 | all-reduce | flops 2048 | bytes 16384 | tf_op jit(solution)/shard_map/psum | solution.py:55
  698.9 10.4 while.101
  698.9 2.6 fusion.155
  701.5 2.6 fusion.155
  704.1 2.6 fusion.155
  706.7 2.6 fusion.155
  709.6 228.3 %reduce-scatter.2.cloned.1.call-done = f32[64,128]{1,0:T(8,128)} async-done(((f32[2048,128]{1,0:T(8,128)}), f32[64,128]{1,0:T(8,128)}) %reduce-scatter.2.cloned.1.call-update) | async-done | bytes 32784 | tf_op jit(solution)/shard_map/reduce_scatter | solution.py:114
  937.9 1.6 fusion.60
  939.5 246.2 %all-reduce.2.cloned.1.call-done = f32[128,128]{1,0:T(8,128)} async-done(((f32[128,128]{1,0:T(8,128)}), f32[128,128]{1,0:T(8,128)}) %all-reduce.2.cloned.1.call-update) | async-done | bytes 65552 | tf_op jit(solution)/shard_map/psum | solution.py:124
  1185.8 1.5 multiply_reduce_fusion
  (192 shorter events, 43.9 us)
Async XLA Ops:
  7.2 1.0 copy-start
  7.2 930.7 %reduce-scatter.2.cloned.1.call-start = ((), (), s32[]{:S(2)}) async-start(), calls=%async_computation.1 | async-start | bytes 1081344 | tf_op jit(solution)/shard_map/reduce_scatter | solution.py:114
  9.4 1.5 copy-start.1
  11.6 1.5 copy-start.1
  13.7 1.5 copy-start.1
  15.9 1.5 copy-start.1
  709.4 476.4 %all-reduce.2.cloned.1.call-start = ((), (), s32[]{:S(2)}) async-start(), calls=%async_computation.2 | async-start | bytes 131072 | tf_op jit(solution)/shard_map/psum | solution.py:124
Sparse Core Ops, SparseCore 0:
  709.5 228.3 reduce-scatter.1
  944.0 241.7 all-reduce.1
where the time goes:
time: 1200 us
  blocking collectives  628 us (52%)
  waiting for transfers between devices  475 us (40%)
  matrix products  60.8 us (5%)
  other arithmetic  18 us (2%)
  between operations  15.3 us (1%)
    psum x1, waiting for transfers between devices, shards(): covariance_sum = lax.psum(partial_value, ('src', 'tgt'))  246 us
    pmax x4, blocking collectives, across_targets(): global_peak = lax.pmax(peak_val, 'tgt')  242 us
    reduce_scatter x1, waiting for transfers between devices, shards(): lax.psum_scatter(parts_out.reshape(rows_here * lax.axis_size('tgt'), widt...  228 us
    psum x4, blocking collectives, across_targets(): totals = lax.psum(totals * jnp.exp(peak_val - global_peak), 'tgt')  228 us
    pmax x3, blocking collectives, across_sources(): global_peak = lax.pmax(peak_val, 'src')  121 us
    psum x3, blocking collectives, across_sources(): totals = lax.psum(totals * jnp.exp(peak_val - global_peak), 'src')  37.1 us
  transfers between devices with their start and end apart: 2, of which 2 were waited for; matrix products, arithmetic and copies ran while one was open for 0% of the time, Pallas kernels for 0%

commit v1 on v0

--- a/solution.py
+++ b/solution.py
@@ -52,7 +52,7 @@
 
 def across_targets(peak_val, totals):
     global_peak = lax.pmax(peak_val, "tgt")
-    totals = lax.psum(totals * jnp.exp(peak_val - global_peak), "tgt")
+    totals = jnp.sum(lax.all_gather(totals * jnp.exp(peak_val - global_peak), "tgt"), axis=0)
     peak_val = global_peak
     return peak_val + jnp.log(totals)
 

time: 1200 us -> 1110 us (0.925)
  blocking collectives: 628 us -> 532 us
    psum x4 -> x0, blocking collectives: 228 us -> none  [across_targets(): totals = lax.psum(totals * jnp.exp(peak_val - global_peak), 'tgt')]
    all_gather x0 -> x4, blocking collectives: none -> 137 us  [across_targets(): lax.all_gather(totals * jnp.exp(peak_val - global_peak), 'tgt')]
where the time goes in v1:
time: 1110 us
  blocking collectives  532 us (48%)
  waiting for transfers between devices  476 us (43%)
  matrix products  60.9 us (5%)
  other arithmetic  18.2 us (2%)
  between operations  15.3 us (1%)
    psum x1, waiting for transfers between devices, shards(): covariance_sum = lax.psum(partial_value, ('src', 'tgt'))  246 us
    pmax x4, blocking collectives, across_targets(): global_peak = lax.pmax(peak_val, 'tgt')  243 us
    reduce_scatter x1, waiting for transfers between devices, shards(): lax.psum_scatter(parts_out.reshape(rows_here * lax.axis_size('tgt'), widt...  230 us
    all_gather x4, blocking collectives, across_targets(): lax.all_gather(totals * jnp.exp(peak_val - global_peak), 'tgt')  137 us
    pmax x3, blocking collectives, across_sources(): global_peak = lax.pmax(peak_val, 'src')  115 us
    psum x3, blocking collectives, across_sources(): totals = lax.psum(totals * jnp.exp(peak_val - global_peak), 'src')  37.1 us
    dot_general x16, matrix products, row_one_block(): jnp.einsum('rd,cd->rc', row_block, target, preferred_element_type=jnp.flo...  23.6 us
  transfers between devices with their start and end apart: 2, of which 2 were waited for; matrix products, arithmetic and copies ran while one was open for 0% of the time, Pallas kernels for 0%

profile of v1, /device:TPU:1, one launch (start us, length us, event | category | flops | bytes accessed | tf_op | source)
XLA Modules:
  0.0 1107.6 jit_solution(6421580594281398857)
XLA Ops:
  9.4 8.7 while.94
  9.4 1.5 fusion.139
  11.6 1.5 fusion.139
  13.7 1.5 fusion.139
  15.9 1.5 fusion.139
  18.1 65.3 %pmax.49 = f32[2048]{0:T(1024)S(1)} all-reduce(f32[2048]{0:T(1024)S(1)} %bitcast.221), channel_id=1, replica_groups=mesh['src'=8,'tgt'=32] {'tgt'}, use_global_device_ids=true, to_apply=%region_4.5 | all-reduce | flops 2048 | bytes 16384 | tf_op jit(solution)/shard_map/pmax | solution.py:54
  83.4 34.1 %all-gather = f32[65536]{0:T(1024)S(1)} all-gather(f32[2048]{0:T(1024)S(1)} %exponential_multiply_fusion.3), channel_id=2, replica_groups=mesh['src'=8,'tgt'=32] {'tgt'}, dimensions={0}, use_global_device_ids=true | all-gather | bytes 270336 | tf_op jit(solution)/shard_map/all_gather | solution.py:55
  117.7 8.4 while.95
  121.9 1.4 fusion.141
  126.1 38.5 %pmax.50 = f32[1024]{0:T(1024)S(1)} all-reduce(f32[1024]{0:T(1024)S(1)} %reduce_max.90), channel_id=1, replica_groups=mesh['src'=8,'tgt'=32] {'src'}, use_global_device_ids=true, to_apply=%region_11.12 | all-reduce | flops 1024 | bytes 8192 | tf_op jit(solution)/shard_map/pmax | solution.py:61
  164.7 12.3 %psum.28 = f32[1024]{0:T(1024)S(1)} all-reduce(f32[1024]{0:T(1024)S(1)} %exponential_multiply_fusion.6), channel_id=1, replica_groups=mesh['src'=8,'tgt'=32] {'src'}, use_global_device_ids=true, to_apply=%region_13.14 | all-reduce | flops 1024 | bytes 8192 | tf_op jit(solution)/shard_map/psum | solution.py:62
  177.0 8.7 while.96
  177.0 1.5 fusion.143
  179.2 1.5 fusion.143
  181.4 1.5 fusion.143
  183.5 1.5 fusion.143
  185.7 59.1 %pmax.51 = f32[2048]{0:T(1024)S(1)} all-reduce(f32[2048]{0:T(1024)S(1)} %bitcast.223), channel_id=1, replica_groups=mesh['src'=8,'tgt'=32] {'tgt'}, use_global_device_ids=true, to_apply=%region_18.19 | all-reduce | flops 2048 | bytes 16384 | tf_op jit(solution)/shard_map/pmax | solution.py:54
  244.9 34.2 %all-gather.1 = f32[65536]{0:T(1024)S(1)} all-gather(f32[2048]{0:T(1024)S(1)} %exponential_multiply_fusion.2), channel_id=3, replica_groups=mesh['src'=8,'tgt'=32] {'tgt'}, dimensions={0}, use_global_device_ids=true | all-gather | bytes 270336 | tf_op jit(solution)/shard_map/all_gather | solution.py:55
  279.2 8.4 while.97
  283.4 1.4 fusion.145
  287.6 38.4 %pmax.52 = f32[1024]{0:T(1024)S(1)} all-reduce(f32[1024]{0:T(1024)S(1)} %reduce_max.91), channel_id=1, replica_groups=mesh['src'=8,'tgt'=32] {'src'}, use_global_device_ids=true, to_apply=%region_25.26 | all-reduce | flops 1024 | bytes 8192 | tf_op jit(solution)/shard_map/pmax | solution.py:61
  326.0 12.4 %psum.29 = f32[1024]{0:T(1024)S(1)} all-reduce(f32[1024]{0:T(1024)S(1)} %exponential_multiply_fusion.5), channel_id=1, replica_groups=mesh['src'=8,'tgt'=32] {'src'}, use_global_device_ids=true, to_apply=%region_27.28 | all-reduce | flops 1024 | bytes 8192 | tf_op jit(solution)/shard_map/psum | solution.py:62
  338.4 8.7 while.98
  338.5 1.5 fusion.147
  340.6 1.5 fusion.147
  342.8 1.5 fusion.147
  345.0 1.5 fusion.147
  347.2 59.1 %pmax.53 = f32[2048]{0:T(1024)S(1)} all-reduce(f32[2048]{0:T(1024)S(1)} %bitcast.225), channel_id=1, replica_groups=mesh['src'=8,'tgt'=32] {'tgt'}, use_global_device_ids=true, to_apply=%region_32.33 | all-reduce | flops 2048 | bytes 16384 | tf_op jit(solution)/shard_map/pmax | solution.py:54
  406.3 34.1 %all-gather.2 = f32[65536]{0:T(1024)S(1)} all-gather(f32[2048]{0:T(1024)S(1)} %exponential_multiply_fusion.1), channel_id=4, replica_groups=mesh['src'=8,'tgt'=32] {'tgt'}, dimensions={0}, use_global_device_ids=true | all-gather | bytes 270336 | tf_op jit(solution)/shard_map/all_gather | solution.py:55
  440.6 8.4 while.99
  449.0 38.4 %pmax.54 = f32[1024]{0:T(1024)S(1)} all-reduce(f32[1024]{0:T(1024)S(1)} %reduce_max.92), channel_id=1, replica_groups=mesh['src'=8,'tgt'=32] {'src'}, use_global_device_ids=true, to_apply=%region_39.40 | all-reduce | flops 1024 | bytes 8192 | tf_op jit(solution)/shard_map/pmax | solution.py:61
  487.4 12.4 %psum.30 = f32[1024]{0:T(1024)S(1)} all-reduce(f32[1024]{0:T(1024)S(1)} %exponential_multiply_fusion.4), channel_id=1, replica_groups=mesh['src'=8,'tgt'=32] {'src'}, use_global_device_ids=true, to_apply=%region_41.42 | all-reduce | flops 1024 | bytes 8192 | tf_op jit(solution)/shard_map/psum | solution.py:62
  500.4 8.7 while.100
  500.4 1.5 fusion.151
  502.6 1.5 fusion.151
  504.8 1.5 fusion.151
  507.0 1.5 fusion.151
  509.2 59.1 %pmax.55 = f32[2048]{0:T(1024)S(1)} all-reduce(f32[2048]{0:T(1024)S(1)} %bitcast.227), channel_id=1, replica_groups=mesh['src'=8,'tgt'=32] {'tgt'}, use_global_device_ids=true, to_apply=%region_46.47 | all-reduce | flops 2048 | bytes 16384 | tf_op jit(solution)/shard_map/pmax | solution.py:54
  568.3 34.3 %all-gather.3 = f32[65536]{0:T(1024)S(1)} all-gather(f32[2048]{0:T(1024)S(1)} %exponential_multiply_fusion), channel_id=5, replica_groups=mesh['src'=8,'tgt'=32] {'tgt'}, dimensions={0}, use_global_device_ids=true | all-gather | bytes 270336 | tf_op jit(solution)/shard_map/all_gather | solution.py:55
  603.3 10.4 while.101
  603.3 2.6 fusion.155
  605.9 2.6 fusion.155
  608.5 2.6 fusion.155
  611.1 2.6 fusion.155
  613.8 229.7 %reduce-scatter.2.cloned.1.call-done = f32[64,128]{1,0:T(8,128)} async-done(((f32[2048,128]{1,0:T(8,128)}), f32[64,128]{1,0:T(8,128)}) %reduce-scatter.2.cloned.1.call-update) | async-done | bytes 32784 | tf_op jit(solution)/shard_map/reduce_scatter | solution.py:114
  843.5 1.6 fusion.60
  845.1 246.0 %all-reduce.2.cloned.1.call-done = f32[128,128]{1,0:T(8,128)} async-done(((f32[128,128]{1,0:T(8,128)}), f32[128,128]{1,0:T(8,128)}) %all-reduce.2.cloned.1.call-update) | async-done | bytes 65552 | tf_op jit(solution)/shard_map/psum | solution.py:124
  1091.1 1.5 multiply_reduce_fusion
  (200 shorter events, 44.0 us)
Async XLA Ops:
  7.2 1.0 copy-start
  7.2 836.3 %reduce-scatter.2.cloned.1.call-start = ((), (), s32[]{:S(2)}) async-start(), calls=%async_computation.1 | async-start | bytes 1081344 | tf_op jit(solution)/shard_map/reduce_scatter | solution.py:114
  9.4 1.5 copy-start.1
  11.6 1.5 copy-start.1
  13.7 1.5 copy-start.1
  15.9 1.5 copy-start.1
  613.7 477.4 %all-reduce.2.cloned.1.call-start = ((), (), s32[]{:S(2)}) async-start(), calls=%async_computation.2 | async-start | bytes 131072 | tf_op jit(solution)/shard_map/psum | solution.py:124
Sparse Core Ops, SparseCore 0:
  613.9 229.5 reduce-scatter.1
  849.6 241.4 all-reduce.1
